TPU v7x, 512 devices: a whole 4x4x16 slice. The times are simulated.
512 devices in a mesh: feat: 8 (over x, core), vert: 64 (over y, z).
Axes of the slice: x: 4, y: 4, z: 16, core: 2. Of those that a mesh axis runs over, the one named last changes fastest.
Arguments:
- features: bfloat16 [512, 131072], P('feat', 'vert'), may hold values from -6 to 6
- tiles: bfloat16 [64, 56, 128, 128], P('vert'), may hold values from -0.375 to 0.375
- tile_rows: int32 [64, 56], P('vert'), may hold values from 0 to 15, as said below
- tile_cols: int32 [64, 56], P('vert'), may hold values from 0 to 1023, as said below
- tile_counts: int32 [64], P('vert'), may hold values from 1 to 56, as said below
- weight: bfloat16 [512, 512], replicated, may hold values from -0.25 to 0.25
- output_gradient: bfloat16 [512, 131072], P(None, ('vert', 'feat')), may hold values from -6 to 6
Outputs:
- activation: bfloat16 [512, 131072], P(None, ('vert', 'feat'))
- weight_gradient: float32 [512, 512], replicated
- feature_grad: bfloat16 [512, 131072], P('feat', 'vert')
Inputs may be any that keep to these rules, and one draw needn't show every extreme that they name: `tile_rows`: slots at or beyond a block's count are unused; their tiles and indices are arbitrary. The block of a column tile, tile_cols // 16, equals the slot's own block or differs from it in exactly one of the lowest 4 bits. `tile_counts`: some block uses all 56 slots.
All inputs are finite; a program needn't handle non-finite values.
Results may differ from a plain program's by a relative error of at most 0.02.
Values may be sent and summed in bfloat16 or wider, within the bound.
A program may use at most 64 MiB of HBM per device.

v0:
```python
import jax
import jax.numpy as jnp
from jax import lax
from jax.sharding import PartitionSpec as P

LEVELS = 4


def partner(shard, axis, stride):
    return lax.ppermute(shard, axis, [(i, i ^ 1 << stride) for i in range(lax.axis_size(axis))])


def fetch_partners(features):
    fetched = []
    for bit in range(LEVELS):
        fetched.append(partner(features, "vert", bit))
    return fetched


def send_partials(remote_terms):
    received = []
    for bit in range(LEVELS):
        outgoing = remote_terms[:, bit].astype(jnp.bfloat16)
        received.append(partner(outgoing, "vert", bit).astype(jnp.float32))
    return received


def tile_products(stacked, level, local, rows, block_tiles, weights, row_tiles):
    picked = stacked[level, :, local]
    share_value = jnp.einsum(
        "cfk,crk->cfr", picked, block_tiles, preferred_element_type=jnp.float32
    )
    indicator_matrix = (rows[None, :] == jnp.arange(row_tiles, dtype=jnp.int32)[:, None]).astype(
        jnp.float32
    ) * weights[None, :]
    reduced_total = jnp.einsum("zy,yqw->qzw", indicator_matrix, share_value)
    return reduced_total.reshape(stacked.shape[1], row_tiles * stacked.shape[3])


def position_summands(share_value, slot_index, groups, feat_local, vdev):
    targets = jnp.arange(groups * (vdev // share_value.shape[2]), dtype=jnp.int32)
    placing = (slot_index[None, :] == targets[:, None]).astype(jnp.float32)
    return jnp.einsum("sc,cfk->fsk", placing, share_value).reshape(feat_local, groups, vdev)


def body(features, tiles, tile_rows, tile_cols, tile_counts, weight, output_gradient):
    feat_local, vdev = features.shape
    tile_side = tiles.shape[2]
    slot_count = tiles.shape[1]
    row_tiles = vdev // tile_side
    my_block = lax.axis_index("vert")
    block_tiles = tiles[0]
    rows = tile_rows[0]
    cols = tile_cols[0]
    differ = jnp.bitwise_xor(cols // row_tiles, my_block)
    level = jnp.zeros(cols.shape, jnp.int32)
    for bit in range(LEVELS):
        level = level + jnp.where(differ == 1 << bit, bit + 1, 0).astype(jnp.int32)
    local = cols % row_tiles
    valid = (jnp.arange(slot_count, dtype=jnp.int32) < tile_counts[0]).astype(jnp.float32)
    stacked = jnp.stack([features] + fetch_partners(features)).reshape(
        LEVELS + 1, feat_local, row_tiles, tile_side
    )
    aggregated = tile_products(stacked, level, local, rows, block_tiles, valid, row_tiles).astype(
        jnp.bfloat16
    )
    full_rows = lax.all_to_all(aggregated, "feat", split_axis=1, concat_axis=0, tiled=True)
    pre = jnp.einsum("io,iv->ov", weight, full_rows, preferred_element_type=jnp.float32)
    sigma = jax.nn.sigmoid(pre)
    activation = (pre * sigma).astype(jnp.bfloat16)
    pre_grad = (output_gradient.astype(jnp.float32) * sigma * (1.0 + pre * (1.0 - sigma))).astype(
        jnp.bfloat16
    )
    weight_term = jnp.einsum("iv,ov->io", full_rows, pre_grad, preferred_element_type=jnp.float32)
    weight_gradient = lax.psum(weight_term, ("feat", "vert"))
    agg_grad = jnp.einsum("io,ov->iv", weight, pre_grad, preferred_element_type=jnp.float32).astype(
        jnp.bfloat16
    )
    grad_cols = lax.all_to_all(agg_grad, "feat", split_axis=0, concat_axis=1, tiled=True)
    picked = grad_cols.reshape(feat_local, row_tiles, tile_side)[:, rows, :]
    share_value = (
        jnp.einsum("fcr,crk->cfk", picked, block_tiles, preferred_element_type=jnp.float32)
        * valid[:, None, None]
    )
    spread = position_summands(share_value, level * row_tiles + local, LEVELS + 1, feat_local, vdev)
    received = send_partials(spread[:, 1:])
    feature_grad = spread[:, 0]
    for term in received:
        feature_grad = feature_grad + term
    return (activation, weight_gradient, feature_grad.astype(jnp.bfloat16))


def solution(mesh):
    in_specs = (
        P("feat", "vert"),
        P("vert", None, None, None),
        P("vert", None),
        P("vert", None),
        P("vert"),
        P(),
        P(None, ("vert", "feat")),
    )
    out_specs = (P(None, ("vert", "feat")), P(), P("feat", "vert"))
    return jax.shard_map(body, mesh=mesh, in_specs=in_specs, out_specs=out_specs, check_vma=False)
```

profile of v0, /device:TPU:1, one launch (start us, length us, event | category | flops | bytes accessed | tf_op | source)
XLA Modules:
  0.0 628.8 jit_solution(14471863540489969215)
XLA Ops:
  7.2 0.0 copy-start
  7.2 5.9 collective-permute-start.1
  13.1 3.5 collective-permute-start
  16.6 12.7 %collective-permute-start.3 = (bf16[64,2048]{1,0:T(8,128)(2,1)}, bf16[64,2048]{1,0:T(8,128)(2,1)S(1)}, u32[]{:S(2)}, u32[]{:S(2)}) collective-permute-start(bf16[64,2048]{1,0:T(8,128)(2,1)} %param.7), channel_id=1, source_target_pairs={{0,8},{1,9},{2,10},{3,11},{4,12},{5,13},{6,14},{7,15},{8,0},{9,1},... | collective-permute-start | bytes 786440 | tf_op jit(solution)/shard_map/ppermute | solution.py:10
  29.4 4.0 collective-permute-start.2
  34.0 0.7 fusion.49
  34.7 1.0 copy.87
  35.7 0.8 copy_dynamic-update-slice_fusion.4
  36.5 0.0 collective-permute-done.1
  36.5 0.0 collective-permute-done
  36.6 10.2 %collective-permute-done.3 = bf16[64,2048]{1,0:T(8,128)(2,1)S(1)} collective-permute-done((bf16[64,2048]{1,0:T(8,128)(2,1)}, bf16[64,2048]{1,0:T(8,128)(2,1)S(1)}, u32[]{:S(2)}, u32[]{:S(2)}) %collective-permute-start.3) | collective-permute-done | bytes 262176 | tf_op jit(solution)/shard_map/ppermute | solution.py:10
  46.9 31.9 %collective-permute-done.2 = bf16[64,2048]{1,0:T(8,128)(2,1)S(1)} collective-permute-done((bf16[64,2048]{1,0:T(8,128)(2,1)}, bf16[64,2048]{1,0:T(8,128)(2,1)S(1)}, u32[]{:S(2)}, u32[]{:S(2)}) %collective-permute-start.2) | collective-permute-done | bytes 262176 | tf_op jit(solution)/shard_map/ppermute | solution.py:10
  78.8 0.8 copy_dynamic-update-slice_fusion.3
  79.5 0.8 copy_dynamic-update-slice_fusion.2
  80.3 0.8 copy_dynamic-update-slice_fusion.1
  81.0 0.8 copy_dynamic-update-slice_fusion
  81.8 2.2 gather_fusion
  84.0 0.0 copy-done
  84.0 0.0 copy-start.3
  84.1 1.4 fusion.2
  85.4 0.0 copy-done.3
  85.4 0.0 copy-start.2
  85.4 0.6 fusion.18
  86.0 0.1 convert_element_type.72
  86.1 0.8 copy.75
  86.9 4.8 all-to-all-start
  91.7 0.0 copy-done.2
  91.7 0.1 copy.76
  91.8 6.3 %all-to-all-done = bf16[64,8,256]{2,0,1:T(8,128)(2,1)S(1)} async-done(((bf16[64,8,256]{2,0,1:T(8,128)(2,1)}), bf16[64,8,256]{2,0,1:T(8,128)(2,1)S(1)}, u32[]{:S(2)}, u32[]{:S(2)}) %all-to-all-start) | async-done | bytes 262176 | tf_op jit(solution)/shard_map/all_to_all | solution.py:67
  98.2 0.0 copy-done.1
  98.2 1.2 multiply_convert_fusion
  99.4 0.3 fusion.17
  99.7 0.8 copy.77
  100.6 4.4 all-to-all-start.1
  104.9 0.0 all-reduce.2.cloned.1.call-start
  105.0 6.5 %all-to-all-done.1 = bf16[8,64,256]{2,1,0:T(8,128)(2,1)S(1)} async-done(((bf16[8,64,256]{2,1,0:T(8,128)(2,1)}), bf16[8,64,256]{2,1,0:T(8,128)(2,1)S(1)}, u32[]{:S(2)}, u32[]{:S(2)}) %all-to-all-start.1) | async-done | bytes 262176 | tf_op jit(solution)/shard_map/all_to_all | solution.py:79
  111.5 0.1 copy.78
  111.6 0.1 reshape.231
  111.7 0.1 copy.79
  111.8 0.7 gather_fusion.1
  112.5 0.6 fusion.11
  113.1 2.4 fusion.8
  115.5 4.4 reshape.232
  119.9 2.5 convert.6
  122.4 1.9 fusion.51
  124.3 0.2 copy.115
  124.5 0.2 copy.112
  124.6 0.9 copy.113
  125.5 0.9 copy.114
  126.3 1.9 collective-permute-start.5
  128.3 1.9 collective-permute-start.6
  130.2 8.5 %collective-permute-start.7 = (bf16[64,2048]{1,0:T(8,128)(2,1)S(1)}, bf16[64,2048]{1,0:T(8,128)(2,1)}, u32[]{:S(2)}, u32[]{:S(2)}) collective-permute-start(bf16[64,2048]{1,0:T(8,128)(2,1)S(1)} %bitcast.108), channel_id=1, source_target_pairs={{0,8},{1,9},{2,10},{3,11},{4,12},{5,13},{6,14},{7,15},{8,0},{9,1},... | collective-permute-start | bytes 786440 | tf_op jit(solution)/shard_map/ppermute | solution.py:10
  138.7 5.8 collective-permute-start.4
  144.5 1.3 fusion.52
  145.8 0.0 all-reduce.2.cloned.1.call-update
  145.8 1.8 copy.81
  147.7 0.0 collective-permute-done.5
  147.7 33.5 %collective-permute-done.6 = bf16[64,2048]{1,0:T(8,128)(2,1)} collective-permute-done((bf16[64,2048]{1,0:T(8,128)(2,1)}, bf16[64,2048]{1,0:T(8,128)(2,1)}, u32[]{:S(2)}, u32[]{:S(2)}) %collective-permute-start.6) | collective-permute-done | bytes 262176 | tf_op jit(solution)/shard_map/ppermute | solution.py:10
  181.1 0.0 collective-permute-done.7
  181.1 0.0 collective-permute-done.4
  181.1 0.0 slice-done
  181.2 2.2 fusion.25
  183.3 436.4 %all-reduce.2.cloned.1.call-done = f32[512,512]{1,0:T(8,128)} async-done(((f32[512,512]{1,0:T(8,128)}), f32[512,512]{1,0:T(8,128)}) %all-reduce.2.cloned.1.call-update) | async-done | bytes 1048592 | tf_op jit(solution)/shard_map/psum | solution.py:75
  619.7 2.3 copy.122
  (12 shorter events, 0.2 us)
Async XLA Ops:
  7.2 76.9 %copy-start = (bf16[1,56,128,128]{3,2,1,0:T(8,128)(2,1)S(1)}, bf16[1,56,128,128]{3,2,1,0:T(8,128)(2,1)}, u32[]{:S(2)}) copy-start(bf16[1,56,128,128]{3,2,1,0:T(8,128)(2,1)} %param.8) | copy-start | bytes 5505028
  7.2 29.3 %collective-permute-start.1 = (bf16[64,2048]{1,0:T(8,128)(2,1)}, bf16[64,2048]{1,0:T(8,128)(2,1)S(1)}, u32[]{:S(2)}, u32[]{:S(2)}) collective-permute-start(bf16[64,2048]{1,0:T(8,128)(2,1)} %param.7), channel_id=1, source_target_pairs={{0,2},{1,3},{2,0},{3,1},{4,6},{5,7},{6,4},{7,5},{8,10},{9,11},{10,... | collective-permute-start | bytes 786440 | tf_op jit(solution)/shard_map/ppermute | solution.py:10
  13.1 23.5 %collective-permute-start = (bf16[64,2048]{1,0:T(8,128)(2,1)}, bf16[64,2048]{1,0:T(8,128)(2,1)S(1)}, u32[]{:S(2)}, u32[]{:S(2)}) collective-permute-start(bf16[64,2048]{1,0:T(8,128)(2,1)} %param.7), channel_id=1, source_target_pairs={{0,1},{1,0},{2,3},{3,2},{4,5},{5,4},{6,7},{7,6},{8,9},{9,8},{10,11... | collective-permute-start | bytes 786440 | tf_op jit(solution)/shard_map/ppermute | solution.py:10
  16.6 30.2 %collective-permute-start.3 = (bf16[64,2048]{1,0:T(8,128)(2,1)}, bf16[64,2048]{1,0:T(8,128)(2,1)S(1)}, u32[]{:S(2)}, u32[]{:S(2)}) collective-permute-start(bf16[64,2048]{1,0:T(8,128)(2,1)} %param.7), channel_id=1, source_target_pairs={{0,8},{1,9},{2,10},{3,11},{4,12},{5,13},{6,14},{7,15},{8,0},{9,1},... | collective-permute-start | bytes 786440 | tf_op jit(solution)/shard_map/ppermute | solution.py:10
  29.4 49.4 %collective-permute-start.2 = (bf16[64,2048]{1,0:T(8,128)(2,1)}, bf16[64,2048]{1,0:T(8,128)(2,1)S(1)}, u32[]{:S(2)}, u32[]{:S(2)}) collective-permute-start(bf16[64,2048]{1,0:T(8,128)(2,1)} %param.7), channel_id=1, source_target_pairs={{0,4},{1,5},{2,6},{3,7},{4,0},{5,1},{6,2},{7,3},{8,12},{9,13},{10,... | collective-permute-start | bytes 786440 | tf_op jit(solution)/shard_map/ppermute | solution.py:10
  84.0 1.4 copy-start.3
  85.4 6.2 copy-start.2
  86.0 12.1 %copy-start.1 = (bf16[512,512]{1,0:T(8,128)(2,1)S(1)}, bf16[512,512]{1,0:T(8,128)(2,1)}, u32[]{:S(2)}) copy-start(bf16[512,512]{1,0:T(8,128)(2,1)} %param.12) | copy-start | bytes 1572868
  86.9 11.3 %all-to-all-start = ((bf16[64,8,256]{2,0,1:T(8,128)(2,1)}), bf16[64,8,256]{2,0,1:T(8,128)(2,1)S(1)}, u32[]{:S(2)}, u32[]{:S(2)}) async-start(bf16[64,8,256]{2,0,1:T(8,128)(2,1)} %copy.75), calls=%async_computation | async-start | bytes 524288 | tf_op jit(solution)/shard_map/all_to_all | solution.py:67
  99.4 5.6 copy-start.4
  100.6 10.9 %all-to-all-start.1 = ((bf16[8,64,256]{2,1,0:T(8,128)(2,1)}), bf16[8,64,256]{2,1,0:T(8,128)(2,1)S(1)}, u32[]{:S(2)}, u32[]{:S(2)}) async-start(bf16[8,64,256]{2,1,0:T(8,128)(2,1)} %bitcast.12), calls=%async_computation.1 | async-start | bytes 524288 | tf_op jit(solution)/shard_map/all_to_all | solution.py:79
  104.9 514.8 %all-reduce.2.cloned.1.call-start = ((), (), s32[]{:S(2)}) async-start(), calls=%async_computation.2 | async-start | bytes 2097152 | tf_op jit(solution)/shard_map/psum | solution.py:75
  126.3 21.3 %collective-permute-start.5 = (bf16[64,2048]{1,0:T(8,128)(2,1)}, bf16[64,2048]{1,0:T(8,128)(2,1)}, u32[]{:S(2)}, u32[]{:S(2)}) collective-permute-start(bf16[64,2048]{1,0:T(8,128)(2,1)} %bitcast.96), channel_id=1, source_target_pairs={{0,2},{1,3},{2,0},{3,1},{4,6},{5,7},{6,4},{7,5},{8,10},{9,11},{10,... | collective-permute-start | bytes 786440 | tf_op jit(solution)/shard_map/ppermute | solution.py:10
  128.3 52.9 %collective-permute-start.6 = (bf16[64,2048]{1,0:T(8,128)(2,1)}, bf16[64,2048]{1,0:T(8,128)(2,1)}, u32[]{:S(2)}, u32[]{:S(2)}) collective-permute-start(bf16[64,2048]{1,0:T(8,128)(2,1)} %bitcast.95), channel_id=1, source_target_pairs={{0,4},{1,5},{2,6},{3,7},{4,0},{5,1},{6,2},{7,3},{8,12},{9,13},{10,... | collective-permute-start | bytes 786440 | tf_op jit(solution)/shard_map/ppermute | solution.py:10
  130.2 50.9 %collective-permute-start.7 = (bf16[64,2048]{1,0:T(8,128)(2,1)S(1)}, bf16[64,2048]{1,0:T(8,128)(2,1)}, u32[]{:S(2)}, u32[]{:S(2)}) collective-permute-start(bf16[64,2048]{1,0:T(8,128)(2,1)S(1)} %bitcast.108), channel_id=1, source_target_pairs={{0,8},{1,9},{2,10},{3,11},{4,12},{5,13},{6,14},{7,15},{8,0},{9,1},... | collective-permute-start | bytes 786440 | tf_op jit(solution)/shard_map/ppermute | solution.py:10
  138.7 42.4 %collective-permute-start.4 = (bf16[64,2048]{1,0:T(8,128)(2,1)S(1)}, bf16[64,2048]{1,0:T(8,128)(2,1)}, u32[]{:S(2)}, u32[]{:S(2)}) collective-permute-start(bf16[64,2048]{1,0:T(8,128)(2,1)S(1)} %bitcast.107), channel_id=1, source_target_pairs={{0,1},{1,0},{2,3},{3,2},{4,5},{5,4},{6,7},{7,6},{8,9},{9,8},{10,11... | collective-permute-start | bytes 786440 | tf_op jit(solution)/shard_map/ppermute | solution.py:10
  145.8 35.3 %slice-start = ((f32[64,5,2048]{2,1,0:T(8,128)}), f32[64,1,2048]{2,1,0:T(1,128)S(1)}, s32[]{:S(2)}) async-start(f32[64,5,2048]{2,1,0:T(8,128)} %reshape.232), calls=%async_computation.3 | async-start | bytes 1048576 | tf_op jit(solution)/shard_map/slice | solution.py:87
Sparse Core Ops, SparseCore 0:
  146.0 473.7 all-reduce.1
where the time goes:
time: 630 us; the launch traced here: 629 us
  waiting for transfers between devices  525 us (83%)
  starting transfers between devices  53.5 us (8%)
  local copies, waits for them, and re-layouts  22.5 us (4%)
  between operations  14.9 us (2%)
  matrix products  7.74 us (1%)
    psum x1, waiting for transfers between devices, body(): weight_gradient = lax.psum(weight_term, ('feat', 'vert'))  436 us
    ppermute x8, waiting for transfers between devices, partner(): lax.ppermute(shard, axis, [(i, i ^ 1 << stride) for i in range(lax.axis_s...  75.5 us
    ppermute x8, starting transfers between devices, partner(): lax.ppermute(shard, axis, [(i, i ^ 1 << stride) for i in range(lax.axis_s...  44.3 us
  transfers between devices with their start and end apart: 11, of which 6 were waited for; matrix products, arithmetic and copies ran while one was open for 1% of the time, Pallas kernels for 0%

commit v1 on v0

--- a/solution.py
+++ b/solution.py
@@ -1,9 +1,19 @@
+import functools
 import jax
 import jax.numpy as jnp
 from jax import lax
 from jax.sharding import PartitionSpec as P
+from jax.lax import psum
 
 LEVELS = 4
+
+
+def recast_area(xin, shard_axis, mesh_ax):
+    out_arr = psum(psum(xin, shard_axis), mesh_ax)
+    return out_arr
+
+
+zone_fill = functools.partial(recast_area, shard_axis="feat", mesh_ax="vert")
 
 
 def partner(shard, axis, stride):
@@ -72,7 +82,7 @@
         jnp.bfloat16
     )
     weight_term = jnp.einsum("iv,ov->io", full_rows, pre_grad, preferred_element_type=jnp.float32)
-    weight_gradient = lax.psum(weight_term, ("feat", "vert"))
+    weight_gradient = zone_fill(weight_term)
     agg_grad = jnp.einsum("io,ov->iv", weight, pre_grad, preferred_element_type=jnp.float32).astype(
         jnp.bfloat16
     )

time: 630 us -> 504 us (0.80); the launches traced: 629 us -> 494 us
  waiting for transfers between devices: 525 us -> 383 us
    psum x1 -> x2, waiting for transfers between devices: 436 us -> 301 us  [recast_area(): out_arr = psum(psum(xin, shard_axis), mesh_ax)]
  transfers between devices with their start and end apart: 11 -> 12, of which waited for: 6 -> 9; matrix products, arithmetic and copies ran while one was open for 1% -> 6% of each run, Pallas kernels for 0% -> 0%
where the time goes in v1:
time: 504 us; the launch traced here: 494 us
  waiting for transfers between devices  383 us (76%)
  starting transfers between devices  54.6 us (11%)
  local copies, waits for them, and re-layouts  26.7 us (5%)
  between operations  15 us (3%)
  matrix products  7.74 us (2%)
  other arithmetic  7.34 us (1%)
    psum x2, waiting for transfers between devices, recast_area(): out_arr = psum(psum(xin, shard_axis), mesh_ax)  301 us
    ppermute x8, waiting for transfers between devices, partner(): lax.ppermute(shard, axis, [(i, i ^ 1 << stride) for i in range(lax.axis_s...  70 us
    ppermute x8, starting transfers between devices, partner(): lax.ppermute(shard, axis, [(i, i ^ 1 << stride) for i in range(lax.axis_s...  45.5 us
    unnamed x26, local copies, waits for them, and re-layouts  10.5 us
  transfers between devices with their start and end apart: 12, of which 9 were waited for; matrix products, arithmetic and copies ran while one was open for 6% of the time, Pallas kernels for 0%

profile of v1, /device:TPU:1, one launch (start us, length us, event | category | flops | bytes accessed | tf_op | source)
XLA Modules:
  0.0 493.9 jit_solution(3093545909105069278)
XLA Ops:
  7.2 0.0 copy-start
  7.2 5.9 %collective-permute-start.1 = (bf16[64,2048]{1,0:T(8,128)(2,1)}, bf16[64,2048]{1,0:T(8,128)(2,1)S(1)}, u32[]{:S(2)}, u32[]{:S(2)}) collective-permute-start(bf16[64,2048]{1,0:T(8,128)(2,1)} %param.7), channel_id=1, source_target_pairs={{0,2},{1,3},{2,0},{3,1},{4,6},{5,7},{6,4},{7,5},{8,10},{9,11},{10,... | collective-permute-start | bytes 786440 | tf_op jit(solution)/shard_map/ppermute | solution.py:20
  13.1 3.5 collective-permute-start
  16.6 12.7 %collective-permute-start.3 = (bf16[64,2048]{1,0:T(8,128)(2,1)}, bf16[64,2048]{1,0:T(8,128)(2,1)S(1)}, u32[]{:S(2)}, u32[]{:S(2)}) collective-permute-start(bf16[64,2048]{1,0:T(8,128)(2,1)} %param.7), channel_id=1, source_target_pairs={{0,8},{1,9},{2,10},{3,11},{4,12},{5,13},{6,14},{7,15},{8,0},{9,1},... | collective-permute-start | bytes 786440 | tf_op jit(solution)/shard_map/ppermute | solution.py:20
  29.4 4.0 collective-permute-start.2
  34.0 0.7 fusion.47
  34.7 0.7 fusion.49
  35.4 1.0 copy.87
  36.4 0.8 copy_dynamic-update-slice_fusion.4
  37.1 0.0 collective-permute-done.1
  37.2 0.0 collective-permute-done
  37.2 9.6 %collective-permute-done.3 = bf16[64,2048]{1,0:T(8,128)(2,1)S(1)} collective-permute-done((bf16[64,2048]{1,0:T(8,128)(2,1)}, bf16[64,2048]{1,0:T(8,128)(2,1)S(1)}, u32[]{:S(2)}, u32[]{:S(2)}) %collective-permute-start.3) | collective-permute-done | bytes 262176 | tf_op jit(solution)/shard_map/ppermute | solution.py:20
  46.9 31.9 %collective-permute-done.2 = bf16[64,2048]{1,0:T(8,128)(2,1)S(1)} collective-permute-done((bf16[64,2048]{1,0:T(8,128)(2,1)}, bf16[64,2048]{1,0:T(8,128)(2,1)S(1)}, u32[]{:S(2)}, u32[]{:S(2)}) %collective-permute-start.2) | collective-permute-done | bytes 262176 | tf_op jit(solution)/shard_map/ppermute | solution.py:20
  78.8 0.8 copy_dynamic-update-slice_fusion.3
  79.5 0.8 copy_dynamic-update-slice_fusion.2
  80.3 0.8 copy_dynamic-update-slice_fusion.1
  81.0 0.8 copy_dynamic-update-slice_fusion
  81.8 2.2 gather_fusion
  84.0 0.0 copy-done
  84.0 0.0 copy-start.3
  84.1 1.4 fusion.2
  85.4 0.0 copy-done.3
  85.4 0.0 copy-start.2
  85.4 0.6 fusion.18
  86.0 0.1 convert_element_type.72
  86.1 0.8 copy.75
  86.9 4.8 all-to-all-start
  91.7 0.1 copy.76
  91.9 6.3 %all-to-all-done = bf16[64,8,256]{2,0,1:T(8,128)(2,1)S(1)} async-done(((bf16[64,8,256]{2,0,1:T(8,128)(2,1)}), bf16[64,8,256]{2,0,1:T(8,128)(2,1)S(1)}, u32[]{:S(2)}, u32[]{:S(2)}) %all-to-all-start) | async-done | bytes 262176 | tf_op jit(solution)/shard_map/all_to_all | solution.py:77
  98.2 1.2 multiply_convert_fusion
  99.4 0.3 fusion.17
  99.7 0.8 copy.77
  100.6 4.4 all-to-all-start.1
  104.9 1.3 fusion.52
  106.2 0.0 all-reduce.3.cloned.1.call-update
  106.2 0.0 all-reduce.5.cloned.1.call-start
  106.3 5.2 %all-to-all-done.1 = bf16[8,64,256]{2,1,0:T(8,128)(2,1)S(1)} async-done(((bf16[8,64,256]{2,1,0:T(8,128)(2,1)}), bf16[8,64,256]{2,1,0:T(8,128)(2,1)S(1)}, u32[]{:S(2)}, u32[]{:S(2)}) %all-to-all-start.1) | async-done | bytes 262176 | tf_op jit(solution)/shard_map/all_to_all | solution.py:89
  111.5 0.1 copy.78
  111.6 0.1 reshape.231
  111.7 0.1 copy.79
  111.8 0.7 gather_fusion.1
  112.5 0.6 fusion.11
  113.1 2.4 fusion.8
  115.5 4.4 reshape.232
  119.9 4.0 convert.6
  123.8 57.1 %all-reduce.3.cloned.1.call-done = f32[512,512]{1,0:T(8,128)} async-done(((f32[512,512]{1,0:T(8,128)}), f32[512,512]{1,0:T(8,128)}) %all-reduce.3.cloned.1.call-update) | async-done | bytes 1048592 | tf_op jit(solution)/shard_map/psum | solution.py:12
  180.9 0.0 all-reduce.5.cloned.1.call-update
  180.9 6.2 %fusion.51 = (bf16[64,1,2048]{2,1,0:T(2,128)(2,1)S(1)}, bf16[64,1,2048]{2,1,0:T(2,128)(2,1)S(1)}, bf16[64,1,2048]{2,1,0:T(2,128)(2,1)S(1)}, bf16[64,1,2048]{2,1,0:T(2,128)(2,1)S(1)}) fusion(bf16[64,5,2048]{2,1,0:T(8,128)(2,1)} %convert.6), kind=kLoop, calls=%fused_computation.85 | loop fusion | bytes 2097152 | tf_op jit(solution)/shard_map/slice | solution.py:33
  187.1 0.2 copy.115
  187.3 0.2 copy.112
  187.5 0.9 copy.113
  188.3 0.9 copy.114
  189.2 3.7 collective-permute-start.5
  192.9 7.4 %collective-permute-start.6 = (bf16[64,2048]{1,0:T(8,128)(2,1)}, bf16[64,2048]{1,0:T(8,128)(2,1)S(1)}, u32[]{:S(2)}, u32[]{:S(2)}) collective-permute-start(bf16[64,2048]{1,0:T(8,128)(2,1)} %bitcast.95), channel_id=1, source_target_pairs={{0,4},{1,5},{2,6},{3,7},{4,0},{5,1},{6,2},{7,3},{8,12},{9,13},{10,... | collective-permute-start | bytes 786440 | tf_op jit(solution)/shard_map/ppermute | solution.py:20
  200.3 5.9 %collective-permute-start.7 = (bf16[64,2048]{1,0:T(8,128)(2,1)S(1)}, bf16[64,2048]{1,0:T(8,128)(2,1)}, u32[]{:S(2)}, u32[]{:S(2)}) collective-permute-start(bf16[64,2048]{1,0:T(8,128)(2,1)S(1)} %bitcast.108), channel_id=1, source_target_pairs={{0,8},{1,9},{2,10},{3,11},{4,12},{5,13},{6,14},{7,15},{8,0},{9,1},... | collective-permute-start | bytes 786440 | tf_op jit(solution)/shard_map/ppermute | solution.py:20
  206.2 2.3 collective-permute-start.4
  208.5 1.8 copy.81
  210.3 9.1 %collective-permute-done.5 = bf16[64,2048]{1,0:T(8,128)(2,1)S(1)} collective-permute-done((bf16[64,2048]{1,0:T(8,128)(2,1)}, bf16[64,2048]{1,0:T(8,128)(2,1)S(1)}, u32[]{:S(2)}, u32[]{:S(2)}) %collective-permute-start.5) | collective-permute-done | bytes 262176 | tf_op jit(solution)/shard_map/ppermute | solution.py:20
  219.4 10.8 %collective-permute-done.6 = bf16[64,2048]{1,0:T(8,128)(2,1)S(1)} collective-permute-done((bf16[64,2048]{1,0:T(8,128)(2,1)}, bf16[64,2048]{1,0:T(8,128)(2,1)S(1)}, u32[]{:S(2)}, u32[]{:S(2)}) %collective-permute-start.6) | collective-permute-done | bytes 262176 | tf_op jit(solution)/shard_map/ppermute | solution.py:20
  230.2 0.0 collective-permute-done.7
  230.2 8.6 %collective-permute-done.4 = bf16[64,2048]{1,0:T(8,128)(2,1)} collective-permute-done((bf16[64,2048]{1,0:T(8,128)(2,1)S(1)}, bf16[64,2048]{1,0:T(8,128)(2,1)}, u32[]{:S(2)}, u32[]{:S(2)}) %collective-permute-start.4) | collective-permute-done | bytes 262176 | tf_op jit(solution)/shard_map/ppermute | solution.py:20
  238.9 2.0 fusion.25
  240.9 243.9 %all-reduce.5.cloned.1.call-done = f32[512,512]{1,0:T(8,128)} async-done(((f32[512,512]{1,0:T(8,128)}), f32[512,512]{1,0:T(8,128)}) %all-reduce.5.cloned.1.call-update) | async-done | bytes 1048592 | tf_op jit(solution)/shard_map/psum | solution.py:12
  484.8 2.3 copy.123
  (15 shorter events, 0.2 us)
Async XLA Ops:
  7.2 76.9 %copy-start = (bf16[1,56,128,128]{3,2,1,0:T(8,128)(2,1)S(1)}, bf16[1,56,128,128]{3,2,1,0:T(8,128)(2,1)}, u32[]{:S(2)}) copy-start(bf16[1,56,128,128]{3,2,1,0:T(8,128)(2,1)} %param.8) | copy-start | bytes 5505028
  7.2 30.0 %collective-permute-start.1 = (bf16[64,2048]{1,0:T(8,128)(2,1)}, bf16[64,2048]{1,0:T(8,128)(2,1)S(1)}, u32[]{:S(2)}, u32[]{:S(2)}) collective-permute-start(bf16[64,2048]{1,0:T(8,128)(2,1)} %param.7), channel_id=1, source_target_pairs={{0,2},{1,3},{2,0},{3,1},{4,6},{5,7},{6,4},{7,5},{8,10},{9,11},{10,... | collective-permute-start | bytes 786440 | tf_op jit(solution)/shard_map/ppermute | solution.py:20
  13.1 24.1 %collective-permute-start = (bf16[64,2048]{1,0:T(8,128)(2,1)}, bf16[64,2048]{1,0:T(8,128)(2,1)S(1)}, u32[]{:S(2)}, u32[]{:S(2)}) collective-permute-start(bf16[64,2048]{1,0:T(8,128)(2,1)} %param.7), channel_id=1, source_target_pairs={{0,1},{1,0},{2,3},{3,2},{4,5},{5,4},{6,7},{7,6},{8,9},{9,8},{10,11... | collective-permute-start | bytes 786440 | tf_op jit(solution)/shard_map/ppermute | solution.py:20
  16.6 30.2 %collective-permute-start.3 = (bf16[64,2048]{1,0:T(8,128)(2,1)}, bf16[64,2048]{1,0:T(8,128)(2,1)S(1)}, u32[]{:S(2)}, u32[]{:S(2)}) collective-permute-start(bf16[64,2048]{1,0:T(8,128)(2,1)} %param.7), channel_id=1, source_target_pairs={{0,8},{1,9},{2,10},{3,11},{4,12},{5,13},{6,14},{7,15},{8,0},{9,1},... | collective-permute-start | bytes 786440 | tf_op jit(solution)/shard_map/ppermute | solution.py:20
  29.4 49.4 %collective-permute-start.2 = (bf16[64,2048]{1,0:T(8,128)(2,1)}, bf16[64,2048]{1,0:T(8,128)(2,1)S(1)}, u32[]{:S(2)}, u32[]{:S(2)}) collective-permute-start(bf16[64,2048]{1,0:T(8,128)(2,1)} %param.7), channel_id=1, source_target_pairs={{0,4},{1,5},{2,6},{3,7},{4,0},{5,1},{6,2},{7,3},{8,12},{9,13},{10,... | collective-permute-start | bytes 786440 | tf_op jit(solution)/shard_map/ppermute | solution.py:20
  84.0 1.4 copy-start.3
  85.4 6.3 %copy-start.2 = (bf16[512,256]{1,0:T(8,128)(2,1)S(1)}, bf16[512,256]{1,0:T(8,128)(2,1)}, u32[]{:S(2)}) copy-start(bf16[512,256]{1,0:T(8,128)(2,1)} %param.13) | copy-start | bytes 786436
  86.0 5.8 %copy-start.4 = (s32[1,56]{1,0:T(1,128)S(1)}, s32[1,56]{1,0:T(1,128)}, u32[]{:S(2)}) copy-start(s32[1,56]{1,0:T(1,128)} %param.10) | copy-start | bytes 676
  86.0 12.2 %copy-start.1 = (bf16[512,512]{1,0:T(8,128)(2,1)S(1)}, bf16[512,512]{1,0:T(8,128)(2,1)}, u32[]{:S(2)}) copy-start(bf16[512,512]{1,0:T(8,128)(2,1)} %param.12) | copy-start | bytes 1572868
  86.9 11.3 %all-to-all-start = ((bf16[64,8,256]{2,0,1:T(8,128)(2,1)}), bf16[64,8,256]{2,0,1:T(8,128)(2,1)S(1)}, u32[]{:S(2)}, u32[]{:S(2)}) async-start(bf16[64,8,256]{2,0,1:T(8,128)(2,1)} %copy.75), calls=%async_computation | async-start | bytes 524288 | tf_op jit(solution)/shard_map/all_to_all | solution.py:77
  100.6 10.9 %all-to-all-start.1 = ((bf16[8,64,256]{2,1,0:T(8,128)(2,1)}), bf16[8,64,256]{2,1,0:T(8,128)(2,1)S(1)}, u32[]{:S(2)}, u32[]{:S(2)}) async-start(bf16[8,64,256]{2,1,0:T(8,128)(2,1)} %bitcast.12), calls=%async_computation.1 | async-start | bytes 524288 | tf_op jit(solution)/shard_map/all_to_all | solution.py:89
  104.9 76.0 %all-reduce.3.cloned.1.call-start = ((), (), s32[]{:S(2)}) async-start(), calls=%async_computation.2 | async-start | bytes 2097152 | tf_op jit(solution)/shard_map/psum | solution.py:12
  106.2 378.6 %all-reduce.5.cloned.1.call-start = ((), (), s32[]{:S(2)}) async-start(), calls=%async_computation.3 | async-start | bytes 2097152 | tf_op jit(solution)/shard_map/psum | solution.py:12
  188.3 50.5 %slice-start = ((f32[64,5,2048]{2,1,0:T(8,128)}), f32[64,1,2048]{2,1,0:T(1,128)S(1)}, s32[]{:S(2)}) async-start(f32[64,5,2048]{2,1,0:T(8,128)} %reshape.232), calls=%async_computation.4 | async-start | bytes 1048576 | tf_op jit(solution)/shard_map/slice | solution.py:97
  189.2 30.2 %collective-permute-start.5 = (bf16[64,2048]{1,0:T(8,128)(2,1)}, bf16[64,2048]{1,0:T(8,128)(2,1)S(1)}, u32[]{:S(2)}, u32[]{:S(2)}) collective-permute-start(bf16[64,2048]{1,0:T(8,128)(2,1)} %bitcast.96), channel_id=1, source_target_pairs={{0,2},{1,3},{2,0},{3,1},{4,6},{5,7},{6,4},{7,5},{8,10},{9,11},{10,... | collective-permute-start | bytes 786440 | tf_op jit(solution)/shard_map/ppermute | solution.py:20
  192.9 37.3 %collective-permute-start.6 = (bf16[64,2048]{1,0:T(8,128)(2,1)}, bf16[64,2048]{1,0:T(8,128)(2,1)S(1)}, u32[]{:S(2)}, u32[]{:S(2)}) collective-permute-start(bf16[64,2048]{1,0:T(8,128)(2,1)} %bitcast.95), channel_id=1, source_target_pairs={{0,4},{1,5},{2,6},{3,7},{4,0},{5,1},{6,2},{7,3},{8,12},{9,13},{10,... | collective-permute-start | bytes 786440 | tf_op jit(solution)/shard_map/ppermute | solution.py:20
  200.3 30.0 %collective-permute-start.7 = (bf16[64,2048]{1,0:T(8,128)(2,1)S(1)}, bf16[64,2048]{1,0:T(8,128)(2,1)}, u32[]{:S(2)}, u32[]{:S(2)}) collective-permute-start(bf16[64,2048]{1,0:T(8,128)(2,1)S(1)} %bitcast.108), channel_id=1, source_target_pairs={{0,8},{1,9},{2,10},{3,11},{4,12},{5,13},{6,14},{7,15},{8,0},{9,1},... | collective-permute-start | bytes 786440 | tf_op jit(solution)/shard_map/ppermute | solution.py:20
  206.2 32.6 %collective-permute-start.4 = (bf16[64,2048]{1,0:T(8,128)(2,1)S(1)}, bf16[64,2048]{1,0:T(8,128)(2,1)}, u32[]{:S(2)}, u32[]{:S(2)}) collective-permute-start(bf16[64,2048]{1,0:T(8,128)(2,1)S(1)} %bitcast.107), channel_id=1, source_target_pairs={{0,1},{1,0},{2,3},{3,2},{4,5},{5,4},{6,7},{7,6},{8,9},{9,8},{10,11... | collective-permute-start | bytes 786440 | tf_op jit(solution)/shard_map/ppermute | solution.py:20
Sparse Core Ops, SparseCore 0:
  108.7 72.1 all-reduce.2
  184.3 300.4 all-reduce.4
